TPU v7x, 1024 devices: a whole 4x8x16 slice. The times are simulated.
1024 devices in a mesh: section: 16 (over y, core), expert: 64 (over z, x).
Axes of the slice: x: 4, y: 8, z: 16, core: 2. Of those that a mesh axis runs over, the one named last changes fastest.
Arguments:
- held: bfloat16 [16, 8192, 3584], P('section', 'expert'), may hold values from -0.59765625 to 0.59765625
- incoming: bfloat16 [1, 8192, 3584], P(None, 'expert'), may hold values from -0.59765625 to 0.59765625
- route_ids: int32 [2, 16, 8192, 8], P(None, 'section', 'expert'), may hold values from 0 to 255, all different within a row; in each aligned block of 128 rows (0 to 127, 128 to 255, ..., all dimensions but the last counted through in order) at most 4 rows name the same one
- gain: bfloat16 [16, 3584], P('section'), may hold values from 0.099609375 to 1.8984375
- router: bfloat16 [16, 3584, 256], P('section'), may hold values from -0.09375 to 0.09375
- w_gate: bfloat16 [16, 4096, 3584], P('section', 'expert'), may hold values from -0.09375 to 0.09375
- w_up: bfloat16 [16, 4096, 3584], P('section', 'expert'), may hold values from -0.09375 to 0.09375
- w_down: bfloat16 [16, 4096, 3584], P('section', 'expert'), may hold values from -0.5 to 0.5
Outputs:
- layer_out: bfloat16 [16, 8192, 3584], P('section', 'expert')
Inputs may be any that keep to these rules, and one draw needn't show every extreme that they name: `route_ids`: each row names 8 different experts. Within the 128 rows of one device at one tick and section, no expert is named by more than 4 rows; some expert is named by exactly 4 rows in some such blocks.
All inputs are finite; a program needn't handle non-finite values.
Results may differ from a plain program's by a relative error of at most 0.0073.
Values may be sent and summed in bfloat16 or wider, within the bound.
A program may use at most 32 MiB of HBM per device.

v0:
```python
import jax
import jax.numpy as jnp
from jax import lax
from jax.sharding import PartitionSpec as P

route_scale = 2.5


def from_behind(value, axis, steps):
    count = lax.axis_size(axis)
    initial, last = (max(0, -steps), min(count, count - steps))
    return lax.ppermute(value, axis, [(source, source + steps) for source in range(initial, last)])


def expert_ffn(received, gate_w, up_w, down_w):
    shape = received.shape
    rows = received.reshape(-1, shape[2])
    dims = (((1,), (1,)), ((), ()))
    gate = lax.dot_general(rows, gate_w, dims, preferred_element_type=jnp.float32)
    upper = lax.dot_general(rows, up_w, dims, preferred_element_type=jnp.float32)
    hidden = (jax.nn.silu(gate) * upper).astype(jnp.bfloat16)
    output = jnp.dot(hidden, down_w, preferred_element_type=jnp.float32).astype(jnp.bfloat16)
    return output.reshape(shape)


def route_layer(state, ids, gain_row, router_w, gate_w, up_w, down_w):
    tok_rows, width = state.shape
    top = ids.shape[1]
    experts = router_w.shape[1]
    n_owner = lax.axis_size("expert")
    sharers = min(16, n_owner)
    flying = n_owner // sharers
    capacity = max(2, tok_rows * top // experts)
    x_val = state.astype(jnp.float32)
    normed = (
        x_val
        * lax.rsqrt(jnp.mean(x_val * x_val, -1, keepdims=True) + 1e-06)
        * gain_row.astype(jnp.float32)
    ).astype(jnp.bfloat16)
    scores = jax.nn.sigmoid(jnp.dot(normed, router_w, preferred_element_type=jnp.float32))
    picked = ids[:, :, None] == lax.broadcasted_iota(jnp.int32, (1, 1, experts), 2)
    chosen = jnp.sum(jnp.where(picked, scores[:, None, :], 0.0), -1)
    weights = route_scale * chosen / jnp.sum(chosen, -1, keepdims=True)
    in_flight = ids[:, :, None] == lax.broadcasted_iota(jnp.int32, (1, 1, flying), 2)
    flat = in_flight.reshape(tok_rows * top, flying).astype(jnp.int32)
    before = jnp.cumsum(flat, 0) - flat
    slot_index = jnp.sum(before * flat, -1)
    position = ids.reshape(-1) * capacity + slot_index
    placed = position[:, None] == lax.broadcasted_iota(jnp.int32, (1, flying * capacity), 1)
    placed = placed.reshape(tok_rows, top, flying * capacity)
    token_place = jnp.sum(placed.astype(jnp.float32), 1).astype(jnp.bfloat16)
    weighted_place = jnp.sum(jnp.where(placed, weights[:, :, None], 0.0), 1)
    compact = lax.dot_general(
        token_place, normed, (((0,), (0,)), ((), ())), preferred_element_type=jnp.float32
    )
    compact = compact.astype(jnp.bfloat16).reshape(flying, 1, capacity, width)
    outgoing = jnp.broadcast_to(compact, (flying, sharers, capacity, width)).reshape(
        n_owner, capacity, width
    )
    finished = expert_ffn(
        lax.all_to_all(outgoing, "expert", split_axis=0, concat_axis=0, tiled=True),
        gate_w,
        up_w,
        down_w,
    )
    returned = lax.all_to_all(finished, "expert", split_axis=0, concat_axis=0, tiled=True)
    summed = jnp.sum(returned.reshape(flying, sharers, capacity, width).astype(jnp.float32), 1)
    combined = jnp.dot(
        weighted_place, summed.reshape(flying * capacity, width), precision=lax.Precision.HIGHEST
    )
    return (x_val + combined).astype(jnp.bfloat16)


def body(held, incoming, route_ids, gain, router, w_gate, w_up, w_down):
    section_index = lax.axis_index("section")
    state = held[0]
    output = state
    ticks = route_ids.shape[0]
    for tick in range(ticks):
        if tick > 0:
            moved = from_behind(output, "section", 1)
            state = jnp.where(section_index == 0, incoming[tick - 1], moved)
        output = route_layer(
            state, route_ids[tick, 0], gain[0], router[0], w_gate[0], w_up[0], w_down[0]
        )
    return output[None]


def solution(mesh):
    return jax.shard_map(
        body,
        mesh=mesh,
        in_specs=(
            P("section", "expert", None),
            P(None, "expert", None),
            P(None, "section", "expert", None),
            P("section", None),
            P("section", None, None),
            P("section", "expert", None),
            P("section", "expert", None),
            P("section", "expert", None),
        ),
        out_specs=P("section", "expert", None),
        check_vma=False,
    )
```

profile of v0, /device:TPU:24, one launch (start us, length us, event | category | flops | bytes accessed | tf_op | source)
XLA Modules:
  0.0 464.7 jit_solution(7482490326068078923)
XLA Ops:
  0.0 0.8 fusion.86
  0.8 0.1 copy.27
  0.9 0.1 eq.114
  1.0 0.1 eq.110
  1.1 1.4 fusion.5
  2.6 0.8 convert_reduce_fusion.4
  3.4 1.1 reduce-window.14
  4.5 0.2 slice_reduce_fusion.1
  4.7 0.2 reduce-window.15
  4.9 0.1 add_bitcast_fusion.1
  5.0 0.1 reduce_sum.131
  5.2 1.7 fusion.26
  6.9 2.0 select_reduce_fusion.2
  9.0 0.4 convolution_convert_fusion.3
  9.5 0.5 broadcast_in_dim.70
  10.0 111.1 %all_to_all.20 = bf16[64,4,3584]{2,1,0:T(4,128)(2,1)} all-to-all(bf16[64,4,3584]{2,1,0:T(4,128)(2,1)S(1)} %bitcast.129), channel_id=1, replica_groups=mesh['section'=16,'expert'=64] {'expert'}, dimensions={0} | all-to-all | bytes 3670016 | tf_op jit(solution)/shard_map/all_to_all | solution.py:61
  121.1 4.0 reshape.181
  125.1 2.3 fusion.58
  127.4 5.0 %convolution_convert_fusion.1 = bf16[256,3584]{1,0:T(8,128)(2,1)} fusion(bf16[256,3584]{1,0:T(8,128)(2,1)} %reshape.181, bf16[1,64,3584]{2,1,0:T(8,128)(2,1)S(1)} %copy-done.2, bf16[1,64,3584]{2,1,0:T(8,128)(2,1)} %param.14, f32[256,64]{0,1:T(8,128)S(1)} %fusion.58), kind=kOutput, calls=%fused_computation.1 | convolution fusion | flops 235896832 | bytes 4653056 | tf_op jit(solution)/shard_map/dot_general | solution.py:22
  132.4 4.1 reshape.182
  136.5 94.3 %all_to_all.21 = bf16[64,4,3584]{2,1,0:T(4,128)(2,1)S(1)} all-to-all(bf16[64,4,3584]{2,1,0:T(4,128)(2,1)} %reshape.182), channel_id=1, replica_groups=mesh['section'=16,'expert'=64] {'expert'}, dimensions={0} | all-to-all | bytes 3670016 | tf_op jit(solution)/shard_map/all_to_all | solution.py:66
  230.8 1.5 convert_reduce_fusion.1
  232.2 1.0 reshape.183
  233.3 2.6 fusion
  235.9 2.1 collective-permute-start
  238.0 0.1 copy.28
  238.1 0.1 eq.128
  238.2 0.1 eq.124
  238.3 1.1 reduce-window.16
  239.4 0.2 slice_reduce_fusion
  239.6 0.2 reduce-window.19
  239.8 0.1 add_bitcast_fusion
  239.9 0.1 reduce_sum.139
  240.1 10.8 %collective-permute-done = bf16[128,3584]{1,0:T(8,128)(2,1)} collective-permute-done((bf16[128,3584]{1,0:T(8,128)(2,1)}, bf16[128,3584]{1,0:T(8,128)(2,1)}, u32[]{:S(2)}, u32[]{:S(2)}) %collective-permute-start) | collective-permute-done | bytes 917536 | tf_op jit(solution)/shard_map/ppermute | solution.py:12
  250.9 1.9 fusion.10
  252.8 0.5 fusion.38
  253.2 2.0 select_reduce_fusion
  255.4 0.4 convolution_convert_fusion.2
  255.8 0.5 broadcast_in_dim.74
  256.3 95.3 %all_to_all.22 = bf16[64,4,3584]{2,1,0:T(4,128)(2,1)} all-to-all(bf16[64,4,3584]{2,1,0:T(4,128)(2,1)S(1)} %bitcast.130), channel_id=1, replica_groups=mesh['section'=16,'expert'=64] {'expert'}, dimensions={0} | all-to-all | bytes 3670016 | tf_op jit(solution)/shard_map/all_to_all | solution.py:61
  351.6 4.0 reshape.186
  355.6 2.2 fusion.56
  357.8 5.0 %convolution_convert_fusion = bf16[256,3584]{1,0:T(8,128)(2,1)} fusion(bf16[256,3584]{1,0:T(8,128)(2,1)} %reshape.186, bf16[1,64,3584]{2,1,0:T(8,128)(2,1)S(1)} %copy-done.2, bf16[1,64,3584]{2,1,0:T(8,128)(2,1)} %param.14, f32[256,64]{0,1:T(8,128)S(1)} %fusion.56), kind=kOutput, calls=%fused_computation | convolution fusion | flops 235896832 | bytes 4653056 | tf_op jit(solution)/shard_map/dot_general | solution.py:22
  362.8 4.1 reshape.187
  366.9 94.3 %all_to_all.23 = bf16[64,4,3584]{2,1,0:T(4,128)(2,1)S(1)} all-to-all(bf16[64,4,3584]{2,1,0:T(4,128)(2,1)} %reshape.187), channel_id=1, replica_groups=mesh['section'=16,'expert'=64] {'expert'}, dimensions={0} | all-to-all | bytes 3670016 | tf_op jit(solution)/shard_map/all_to_all | solution.py:66
  461.3 0.8 convert_reduce_fusion
  462.0 0.1 reshape.188
  462.1 2.6 fusion.2
  (24 shorter events, 0.5 us)
Async XLA Ops:
  0.0 5.2 %copy-start = (bf16[1,3584,256]{2,1,0:T(8,128)(2,1)S(1)}, bf16[1,3584,256]{2,1,0:T(8,128)(2,1)}, u32[]{:S(2)}) copy-start(bf16[1,3584,256]{2,1,0:T(8,128)(2,1)} %param.12) | copy-start | bytes 5505028
  5.2 3.9 copy-start.1
  125.1 2.3 copy-start.2
  235.9 15.0 %collective-permute-start = (bf16[128,3584]{1,0:T(8,128)(2,1)}, bf16[128,3584]{1,0:T(8,128)(2,1)}, u32[]{:S(2)}, u32[]{:S(2)}) collective-permute-start(bf16[128,3584]{1,0:T(8,128)(2,1)} %fusion), channel_id=1, source_target_pairs={{0,64},{64,128},{128,192},{192,256},{256,320},{320,384},{384,448},... | collective-permute-start | bytes 2752520 | tf_op jit(solution)/shard_map/ppermute | solution.py:12
where the time goes:
time: 466 us; the launch traced here: 465 us
  blocking collectives  395 us (85%)
  matrix products  22.7 us (5%)
  local copies, waits for them, and re-layouts  20.5 us (4%)
  other arithmetic  13.3 us (3%)
  waiting for transfers between devices  10.8 us (2%)
    all_to_all x2, blocking collectives, route_layer(): lax.all_to_all(outgoing, 'expert', split_axis=0, concat_axis=0, tiled=True)  206 us
    all_to_all x2, blocking collectives, route_layer(): lax.all_to_all(finished, 'expert', split_axis=0, concat_axis=0, tiled=True)  189 us
    ppermute x1, waiting for transfers between devices, from_behind(): lax.ppermute(value, axis, [(source, source + steps) for source in range(i...  10.8 us
    dot_general x2, matrix products, expert_ffn(): jnp.dot(hidden, down_w, preferred_element_type=jnp.float32)  9.99 us
  transfers between devices with their start and end apart: 1, of which 1 were waited for; matrix products, arithmetic and copies ran while one was open for 0% of the time, Pallas kernels for 0%

commit v1 on v0

v1 whole, which is shorter than its diff:
```python
import jax
import jax.numpy as jnp
from jax import lax
from jax.experimental import pallas as pl
from jax.experimental.pallas import tpu as pltpu
from jax.sharding import PartitionSpec as P

MESH = pl.DeviceIdType.MESH
F32 = jnp.float32
BF16 = jnp.bfloat16

SCALE = 2.5
D = 3584
TOK = 128
TOP = 8
CAP = 4
SLOTS = 16
UNITS = 64
NZ = 16
SUB = 4
DS = D // SUB
LB = DS // 128
EXPERTS = 256
NSEC = 16

S_LOCAL, S_WGU, S_WD, S_X, S_IDS, S_Y = 0, 1, 2, 3, 4, 5
S_TICK = 6
N_SEM = S_TICK + 12
L_X, L_IDS, L_GAIN, L_ROUTER, L_WGU, L_WD, L_OUT = range(7)


def nt(a, b):
    return lax.dot_general(a, b, (((1,), (1,)), ((), ())), preferred_element_type=F32)


def nn(a, b):
    return jnp.dot(a, b, preferred_element_type=F32)


def iota(shape, dim):
    return lax.broadcasted_iota(jnp.int32, shape, dim)


def swap_halves(a):
    return pltpu.roll(a, 4, a.ndim - 2)


def one_hot(flag):
    return jnp.where(flag, 1.0, 0.0).astype(BF16)


def halves(a):
    high = a.astype(BF16)
    low = (a - high.astype(F32)).astype(BF16)
    return jnp.concatenate([high, low], 0)


def placing(ids):
    ids_f = ids.astype(F32).astype(BF16)
    eye = one_hot(iota((TOP, TOP), 0) == iota((TOP, TOP), 1))
    ids_t = nt(eye, ids_f)
    expert_of = (iota((SLOTS, TOK), 0) // CAP).astype(F32)
    hit = jnp.zeros((SLOTS, TOK), F32)
    for k in range(TOP):
        hit = jnp.where(ids_t[k : k + 1, :] == expert_of, 1.0, hit)
    earlier = one_hot(iota((TOK, TOK), 0) < iota((TOK, TOK), 1))
    before = nn(hit.astype(BF16), earlier)
    turn = (iota((SLOTS, TOK), 0) % CAP).astype(F32)
    place = jnp.where(before == turn, hit, 0.0).astype(BF16)
    return place, nn(place, ids_f)


def normalize(comp, gain):
    mean = jnp.mean(comp * comp, -1, keepdims=True)
    return (comp * lax.rsqrt(mean + 1e-06) * gain).astype(BF16)


def slot_weights(normed, router, slot_ids):
    scores = jax.nn.sigmoid(nn(normed, router))
    lane = iota((SLOTS, EXPERTS), 1)
    lane_f = lane.astype(F32)
    picked = jnp.zeros((SLOTS, EXPERTS), F32)
    for k in range(TOP):
        picked = jnp.where(slot_ids[:, k : k + 1] == lane_f, 1.0, picked)
    total = jnp.sum(scores * picked, -1, keepdims=True)
    own = jnp.sum(
        jnp.where(lane == iota((SLOTS, EXPERTS), 0) // CAP, scores, 0.0), -1, keepdims=True
    )
    return SCALE * own / total


def kernel(
    held, incoming, ids, gain, router, wg, wu, wd, out,
    xv, xp, idv, idp, gv, rv, wgu, wdv,
    zsend, zrecv, xbuf, rsend, rrecv, guf, hbuf, osend, orecv, of, bsend, brecv,
    ysend, yrecv, b1, ov, comp_s, comp1_s, moe_s,
    loc, snd, rcv,
):
    sec = lax.axis_index("section")
    ex = lax.axis_index("expert")
    z, x = ex // SUB, ex % SUB
    e, zz = z // SUB, z % SUB

    def at_z(other):
        return {"expert": other * SUB + x}

    def at_x(other):
        return {"expert": z * SUB + other}

    after = {"section": (sec + 1) % NSEC}
    before = {"section": (sec + NSEC - 1) % NSEC}

    def local(src, dst, number):
        return pltpu.make_async_copy(src, dst, loc.at[number])

    def send(src, dst, number, device):
        pltpu.make_async_remote_copy(
            src_ref=src, dst_ref=dst, send_sem=snd.at[number], recv_sem=rcv.at[number],
            device_id=device, device_id_type=MESH,
        ).start()

    def arrived(ref, number):
        pltpu.make_async_copy(ref, ref, rcv.at[number]).wait()

    def sent(ref, number):
        pltpu.make_async_copy(ref, ref, snd.at[number]).wait()

    own = pl.ds(pl.multiple_of(zz * DS, 128), DS)
    starts = [
        local(held.at[0], xv, L_X),
        local(ids.at[:, 0], idv, L_IDS),
        local(gain, gv, L_GAIN),
        local(router.at[0], rv, L_ROUTER),
        local(wg.at[0, :, own], wgu.at[0, zz], L_WGU),
        local(wu.at[0, :, own], wgu.at[1, zz], L_WGU),
        local(wd.at[0, :, own], wdv.at[zz], L_WD),
    ]
    for copy in starts:
        copy.start()

    barrier = pltpu.get_barrier_semaphore()

    @pl.loop(1, NZ)
    def _(k):
        pl.semaphore_signal(barrier, inc=1, device_id=at_z((z + k) % NZ), device_id_type=MESH)

    for k in range(1, SUB):
        pl.semaphore_signal(barrier, inc=1, device_id=at_x((x + k) % SUB), device_id_type=MESH)
    pl.semaphore_signal(barrier, inc=1, device_id=after, device_id_type=MESH)
    pl.semaphore_signal(barrier, inc=1, device_id=before, device_id_type=MESH)
    pl.semaphore_wait(barrier, NZ - 1 + SUB - 1 + 2)

    for k in range(1, SUB):
        to = (zz + k) % SUB
        columns = pl.ds(pl.multiple_of(to * DS, 128), DS)
        send(wg.at[0, :, columns], wgu.at[0, zz], S_WGU, at_z(e * SUB + to))
        send(wu.at[0, :, columns], wgu.at[1, zz], S_WGU, at_z(e * SUB + to))

    local(ids.at[:, 0], idv, L_IDS).wait()
    place0, slot_ids0 = placing(idv[0])
    local(gain, gv, L_GAIN).wait()
    gain_row = gv[...].astype(F32)
    local(held.at[0], xv, L_X).wait()
    low4 = iota((1, 8, 128), 1) < 4

    def dispatch(tick, normed):
        rows = normed.astype(F32)
        for part in range(SUB):
            for w in range(2):
                pieces = [[] for _ in range(4)]
                for v in (2 * w, 2 * w + 1):
                    column = (part * LB + 2 * v) * 128
                    a = rows[:, column : column + 128].reshape(2, 8, 128)
                    if 2 * v + 1 < LB:
                        b = rows[:, column + 128 : column + 256].reshape(2, 8, 128)
                    else:
                        b = jnp.zeros((2, 8, 128), F32)
                    even = jnp.where(low4, a, swap_halves(b))
                    odd = jnp.where(low4, swap_halves(a), b)
                    for h in range(2):
                        pieces[2 * h].append(even[h])
                        pieces[2 * h + 1].append(odd[h])
                for n in range(4):
                    zsend[tick, n * SUB + part, 16 * w : 16 * w + 16, :] = jnp.concatenate(
                        pieces[n], 0
                    ).astype(BF16)
        number = S_TICK + 6 * tick

        @pl.loop(1, NZ)
        def _(k):
            to = (z + k) % NZ
            send(zsend.at[tick, to], zrecv.at[tick, z], number, at_z(to))

        zrecv[tick, z] = zsend[tick, z]

    def layer(tick, meanwhile):
        base = S_TICK + 6 * tick
        arrived(zrecv.at[tick, pl.ds(0, NZ - 1)], base)
        got = zrecv[tick].astype(F32).reshape(8, 2, 4, 8, 128)
        for v in range(4):
            a, b = got[:, 0, v], got[:, 1, v]
            even = jnp.where(low4, a, swap_halves(b))
            xbuf[tick, x, :, 2 * v * 128 : (2 * v + 1) * 128] = even.reshape(64, 128).astype(BF16)
            if 2 * v + 1 < LB:
                odd = jnp.where(low4, swap_halves(a), b)
                xbuf[tick, x, :, (2 * v + 1) * 128 : (2 * v + 2) * 128] = odd.reshape(64, 128).astype(BF16)
        for k in range(1, SUB):
            send(xbuf.at[tick, x], xbuf.at[tick, x], base + 1, at_x((x + k) % SUB))
        if tick == 0:
            local(wgu.at[:, zz], wgu.at[:, zz], L_WGU).wait()
            arrived(wgu.at[:, pl.ds(0, SUB - 1)], S_WGU)
        arrived(xbuf.at[tick, pl.ds(0, SUB - 1)], base + 1)
        sums = nt(xbuf[tick].reshape(256, DS), wgu[...].reshape(512, DS))
        sums = sums.reshape(SUB, 64, 512)
        rsend[tick] = sums.astype(BF16)
        guf[...] = sums
        for k in range(1, SUB):
            to = (zz + k) % SUB
            send(rsend.at[tick, to], rrecv.at[tick, zz], base + 2, at_z(e * SUB + to))
        arrived(rrecv.at[tick, pl.ds(0, SUB - 1)], base + 2)
        total = guf[zz]
        for k in range(1, SUB):
            total = total + rrecv[tick, (zz + k) % SUB].astype(F32)
        gate, upper = total[:, :256], total[:, 256:]
        hbuf[tick, zz] = (jax.nn.silu(gate) * upper).astype(BF16)
        for k in range(1, SUB):
            send(hbuf.at[tick, zz], hbuf.at[tick, zz], base + 3, at_z(e * SUB + (zz + k) % SUB))
        if tick == 0:
            local(wd.at[0, :, own], wdv.at[zz], L_WD).wait()
            arrived(wdv.at[pl.ds(0, SUB - 1)], S_WD)
        arrived(hbuf.at[tick, pl.ds(0, SUB - 1)], base + 3)
        product = nn(hbuf[tick].reshape(256, 256), wdv[...].reshape(256, DS))
        product = product.reshape(SUB, 64, DS)
        osend[tick] = product.astype(BF16)
        of[...] = product
        for k in range(1, SUB):
            to = (x + k) % SUB
            send(osend.at[tick, to], orecv.at[tick, x], base + 4, at_x(to))
        arrived(orecv.at[tick, pl.ds(0, SUB - 1)], base + 4)
        total = of[x]
        for k in range(1, SUB):
            total = total + orecv[tick, (x + k) % SUB].astype(F32)
        for w in range(2):
            evens, odds = [], []
            for v in (2 * w, 2 * w + 1):
                a = total[:, 2 * v * 128 : (2 * v + 1) * 128].reshape(8, 8, 128)
                if 2 * v + 1 < LB:
                    b = total[:, (2 * v + 1) * 128 : (2 * v + 2) * 128].reshape(8, 8, 128)
                else:
                    b = jnp.zeros((8, 8, 128), F32)
                evens.append(jnp.where(low4, a, swap_halves(b)))
                odds.append(jnp.where(low4, swap_halves(a), b))
            bsend[tick, :, 0, 16 * w : 16 * w + 16, :] = jnp.concatenate(evens, 1).astype(BF16)
            bsend[tick, :, 1, 16 * w : 16 * w + 16, :] = jnp.concatenate(odds, 1).astype(BF16)

        @pl.loop(1, NZ)
        def _(k):
            to = (z + k) % NZ
            send(bsend.at[tick, to // 2, to % 2], brecv.at[tick, z], base + 5, at_z(to))

        brecv[tick, z] = bsend[tick, z // 2, z % 2]
        meanwhile()
        arrived(brecv.at[tick, pl.ds(0, NZ - 1)], base + 5)
        for half in range(2):
            for part in range(SUB):
                first = brecv[tick, (2 * half) * SUB + part].astype(F32).reshape(4, 8, 128)
                second = brecv[tick, (2 * half + 1) * SUB + part].astype(F32).reshape(4, 8, 128)
                even = jnp.where(low4, first, swap_halves(second))
                odd = jnp.where(low4, swap_halves(first), second)
                for v in range(4):
                    column = (part * LB + 2 * v) * 128
                    moe_s[8 * half : 8 * half + 8, column : column + 128] = even[v]
                    if 2 * v + 1 < LB:
                        moe_s[8 * half : 8 * half + 8, column + 128 : column + 256] = odd[v]
        return moe_s[...]

    comp = nn(place0, xv[...])
    comp_s[...] = comp
    normed = normalize(comp, gain_row)
    dispatch(0, normed)
    for k in range(1, SUB):
        to = (zz + k) % SUB
        columns = pl.ds(pl.multiple_of(to * DS, 128), DS)
        send(wd.at[0, :, columns], wdv.at[zz], S_WD, at_z(e * SUB + to))

    @pl.when(sec == NSEC - 1)
    def _():
        send(incoming.at[0], xp, S_X, after)

    @pl.when(sec != NSEC - 1)
    def _():
        send(held.at[0], xp, S_X, after)

    send(idv.at[0], idp, S_IDS, after)
    local(router.at[0], rv, L_ROUTER).wait()
    weights0 = slot_weights(normed, rv[...], slot_ids0)
    same = nt(place0, place0).astype(BF16)
    same2 = jnp.concatenate([same, same], 1)
    place1, slot_ids1 = placing(idv[1])

    def prepare():
        arrived(idp, S_IDS)
        arrived(xp, S_X)
        prev, _ = placing(idp[...])
        lower = one_hot(iota((SLOTS, SLOTS), 1) < iota((SLOTS, SLOTS), 0))
        seen = nn(lower, prev)
        live = jnp.where(sec == 0, 0.0, 1.0)
        unique = jnp.where(seen == 0.0, prev.astype(F32), 0.0) * live
        touched = jnp.sum(unique, 0, keepdims=True)
        untouched = (place1.astype(F32) * (1.0 - touched)).astype(BF16)
        comp1_s[...] = nn(untouched, xp[...])

    moe = layer(0, prepare)
    y16 = comp_s[...] + nn(same2, halves(moe * weights0))
    ysend[...] = y16.astype(BF16)
    send(ysend, yrecv, S_Y, after)
    prev, _ = placing(idp[...])
    lower = one_hot(iota((SLOTS, SLOTS), 1) < iota((SLOTS, SLOTS), 0))
    live = jnp.where(sec == 0, 0.0, 1.0)
    unique = jnp.where(nn(lower, prev) == 0.0, prev.astype(F32), 0.0) * live
    unique = unique.astype(BF16)
    moved = nt(place1, unique).astype(BF16)
    eye = one_hot(iota((TOK, TOK), 0) == iota((TOK, TOK), 1))
    scatter = nt(eye, unique).astype(BF16)
    combine = nt(eye, jnp.concatenate([place1, place1], 0)).astype(BF16)
    kept = 1.0 - jnp.sum(scatter.astype(F32), 1, keepdims=True)
    arrived(yrecv, S_Y)
    normed = normalize(comp1_s[...] + nn(moved, yrecv[...]), gain_row)
    dispatch(1, normed)
    weights1 = slot_weights(normed, rv[...], slot_ids1)

    def block():
        for part in range(SUB):
            columns = slice(part * DS, (part + 1) * DS)
            b1[:, columns] = xp[:, columns].astype(F32) * kept + nn(scatter, yrecv[:, columns])

    moe = layer(1, block)
    summands = halves(moe * weights1)
    outs = []
    for part in range(SUB):
        columns = slice(part * DS, (part + 1) * DS)
        ov[:, columns] = (b1[:, columns] + nn(combine, summands[:, columns])).astype(BF16)
        copy = local(ov.at[:, columns], out.at[0, :, columns], L_OUT + part)
        copy.start()
        outs.append(copy)
    sent(wgu.at[:, pl.ds(0, SUB - 1)], S_WGU)
    sent(wdv.at[pl.ds(0, SUB - 1)], S_WD)
    sent(xp, S_X)
    sent(idp, S_IDS)
    sent(yrecv, S_Y)
    for tick in range(2):
        base = S_TICK + 6 * tick
        sent(zrecv.at[tick, pl.ds(0, NZ - 1)], base)
        sent(xbuf.at[tick, pl.ds(0, SUB - 1)], base + 1)
        sent(rrecv.at[tick, pl.ds(0, SUB - 1)], base + 2)
        sent(hbuf.at[tick, pl.ds(0, SUB - 1)], base + 3)
        sent(orecv.at[tick, pl.ds(0, SUB - 1)], base + 4)
        sent(brecv.at[tick, pl.ds(0, NZ - 1)], base + 5)
    for copy in outs:
        copy.wait()


def body(held, incoming, route_ids, gain, router, w_gate, w_up, w_down):
    any_space = pl.BlockSpec(memory_space=pl.ANY)
    vm = pltpu.VMEM
    return pl.pallas_call(
        kernel,
        out_shape=jax.ShapeDtypeStruct((1, TOK, D), BF16),
        in_specs=[any_space] * 8,
        out_specs=any_space,
        scratch_shapes=[
            vm((TOK, D), BF16),
            vm((TOK, D), BF16),
            vm((2, TOK, TOP), jnp.int32),
            vm((TOK, TOP), jnp.int32),
            vm((1, D), BF16),
            vm((D, EXPERTS), BF16),
            vm((2, SUB, UNITS, DS), BF16),
            vm((SUB, UNITS, DS), BF16),
            vm((2, NZ, 32, 128), BF16),
            vm((2, NZ, 32, 128), BF16),
            vm((2, SUB, 64, DS), BF16),
            vm((2, SUB, 64, 512), BF16),
            vm((2, SUB, 64, 512), BF16),
            vm((SUB, 64, 512), F32),
            vm((2, SUB, 64, 256), BF16),
            vm((2, SUB, 64, DS), BF16),
            vm((2, SUB, 64, DS), BF16),
            vm((SUB, 64, DS), F32),
            vm((2, 8, 2, 32, 128), BF16),
            vm((2, NZ, 32, 128), BF16),
            vm((SLOTS, D), BF16),
            vm((SLOTS, D), BF16),
            vm((TOK, D), F32),
            vm((TOK, D), BF16),
            vm((SLOTS, D), F32),
            vm((SLOTS, D), F32),
            vm((SLOTS, D), F32),
            pltpu.SemaphoreType.DMA((L_OUT + SUB,)),
            pltpu.SemaphoreType.DMA((N_SEM,)),
            pltpu.SemaphoreType.DMA((N_SEM,)),
        ],
        compiler_params=pltpu.CompilerParams(
            collective_id=0, has_side_effects=True, vmem_limit_bytes=48 * 1024 * 1024
        ),
    )(held, incoming, route_ids, gain, router, w_gate, w_up, w_down)


def solution(mesh):
    return jax.shard_map(
        body,
        mesh=mesh,
        in_specs=(
            P("section", "expert", None),
            P(None, "expert", None),
            P(None, "section", "expert", None),
            P("section", None),
            P("section", None, None),
            P("section", "expert", None),
            P("section", "expert", None),
            P("section", "expert", None),
        ),
        out_specs=P("section", "expert", None),
        check_vma=False,
    )
```

time: 466 us -> 148 us (0.32)
  blocking collectives: 395 us -> 0 us
  Pallas kernels: 0 us -> 138 us
  matrix products: 22.7 us -> 0 us
  other arithmetic: 13.3 us -> 0 us
  local copies, waits for them, and re-layouts: 20.5 us -> 9.36 us
  waiting for transfers between devices: 10.8 us -> 0 us
    all_to_all x4 -> x0, blocking collectives: 395 us -> none  [the longest x2 206 us: route_layer(): lax.all_to_all(outgoing, 'expert', split_axis=0, concat_axis=0, tiled=True)]
    pallas_call x0 -> x1, Pallas kernels: none -> 138 us  [body(): pl.pallas_call(kernel, out_shape=jax.ShapeDtypeStruct((1, TOK, D), BF16),...]
    dot_general x10 -> x0, matrix products: 22.7 us -> none  [the longest x2 9.99 us: expert_ffn(): jnp.dot(hidden, down_w, preferred_element_type=jnp.float32)]
    reshape x6 -> x0, local copies, waits for them, and re-layouts: 17.2 us -> none  [the longest x2 8.21 us: expert_ffn(): return output.reshape(shape)]
    ppermute x1 -> x0, waiting for transfers between devices: 10.8 us -> none  [from_behind(): lax.ppermute(value, axis, [(source, source + steps) for source in range(i...]
    reduce_sum x10 -> x0, other arithmetic: 9.69 us -> none  [the longest x2 4 us: route_layer(): weights = route_scale * chosen / jnp.sum(chosen, -1, keepdims=True)]
    unnamed x8 -> x16, local copies, waits for them, and re-layouts: 0.22 us -> 9.36 us
  transfers between devices with their start and end apart: 1 -> 0, of which waited for: 1 -> 0; matrix products, arithmetic and copies ran while one was open for 0% -> 0% of each run, Pallas kernels for 0% -> 0%
where the time goes in v1:
time: 148 us; the launch traced here: 147 us
  Pallas kernels  138 us (93%)
  local copies, waits for them, and re-layouts  9.36 us (6%)
    pallas_call x1, Pallas kernels, body(): pl.pallas_call(kernel, out_shape=jax.ShapeDtypeStruct((1, TOK, D), BF16),...  138 us
    unnamed x16, local copies, waits for them, and re-layouts  9.36 us

profile of v1, /device:TPU:24, one launch (start us, length us, event | category | flops | bytes accessed | tf_op | source)
XLA Modules:
  0.0 147.1 jit_solution(18274847123706485062)
XLA Ops:
  0.0 0.8 copy.9.ids
  0.8 0.0 copy-start
  0.8 1.5 %copy-done = bf16[1,3584,256]{2,1,0:T(8,128)(2,1)S(1)} copy-done((bf16[1,3584,256]{2,1,0:T(8,128)(2,1)S(1)}, bf16[1,3584,256]{2,1,0:T(8,128)(2,1)}, u32[]{:S(2)}) %copy-start) | copy-done | bytes 1835032
  2.3 0.0 copy-start.1
  2.3 1.2 copy-done.1
  3.5 0.0 copy-start.2
  3.5 1.2 copy-done.2
  4.7 0.0 copy-start.3
  4.7 1.0 copy-done.3
  5.7 0.0 copy-start.4
  5.7 1.0 copy-done.4
  6.7 0.0 copy-start.5
  6.7 1.0 copy-done.5
  7.7 0.0 copy-start.6
  7.7 0.7 copy-done.6
  8.5 137.7 %shard_map.82 = bf16[1,128,3584]{2,1,0:T(8,128)(2,1)S(1)} custom-call(bf16[1,128,3584]{2,1,0:T(8,128)(2,1)S(1)} %copy-done.1, bf16[1,128,3584]{2,1,0:T(8,128)(2,1)S(1)} %copy-done.2, s32[2,1,128,8]{3,2,1,0:T(8,128)S(1)} %copy.9.ids, bf16[1,3584]{1,0:T(2,128)(2,1)S(1)} %copy-done.6, bf16[1,3584,256]{2,1,0:T(8,128)(2,1)S(1)} %copy-done, ...), custom_call_target="tpu_custom_call" | custom-call | tf_op jit(solution)/shard_map/pallas_call | solution.py:366
  146.2 0.9 copy.11
Async XLA Ops:
  0.8 1.5 %copy-start = (bf16[1,3584,256]{2,1,0:T(8,128)(2,1)S(1)}, bf16[1,3584,256]{2,1,0:T(8,128)(2,1)}, u32[]{:S(2)}) copy-start(bf16[1,3584,256]{2,1,0:T(8,128)(2,1)} %router.1) | copy-start | bytes 5505028
  2.3 1.2 copy-start.1
  3.5 1.2 copy-start.2
  4.7 1.0 copy-start.3
  5.7 1.0 copy-start.4
  6.7 1.0 copy-start.5
  7.7 0.7 copy-start.6

commit v2 on v1

v2 whole, which is shorter than its diff:
```python
import jax
import jax.numpy as jnp
from jax import lax
from jax.experimental import pallas as pl
from jax.experimental.pallas import tpu as pltpu
from jax.sharding import PartitionSpec as P

MESH = pl.DeviceIdType.MESH
F32 = jnp.float32
BF16 = jnp.bfloat16

SCALE = 2.5
D = 3584
TOK = 128
TOP = 8
CAP = 4
SLOTS = 16
UNITS = 64
NZ = 16
SUB = 4
DS = D // SUB
LB = DS // 128
EXPERTS = 256
HALF = (0, 512), (512, DS)
BLOCKS = (0, 4), (4, LB)
NSEC = 16

S_WGU, S_WD, S_X, S_IDS, S_Y = 1, 2, 3, 4, 5
S_TICK = 7
PER_TICK = 12
N_SEM = S_TICK + 2 * PER_TICK
L_X, L_IDS, L_GAIN, L_ROUTER, L_WGU, L_WD, L_OUT = range(7)


def nt(a, b):
    return lax.dot_general(a, b, (((1,), (1,)), ((), ())), preferred_element_type=F32)


def nn(a, b):
    return jnp.dot(a, b, preferred_element_type=F32)


def iota(shape, dim):
    return lax.broadcasted_iota(jnp.int32, shape, dim)


def swap_halves(a):
    return pltpu.roll(a, 4, a.ndim - 2)


def one_hot(flag):
    return jnp.where(flag, 1.0, 0.0).astype(BF16)


def halves(a):
    high = a.astype(BF16)
    low = (a - high.astype(F32)).astype(BF16)
    return jnp.concatenate([high, low], 0)


def placing(ids):
    ids_t = ids.astype(F32)
    expert_of = (iota((SLOTS, TOK), 0) // CAP).astype(F32)
    hit = jnp.zeros((SLOTS, TOK), F32)
    for k in range(TOP):
        hit = jnp.where(ids_t[k : k + 1, :] == expert_of, 1.0, hit)
    earlier = one_hot(iota((TOK, TOK), 0) < iota((TOK, TOK), 1))
    before = nn(hit.astype(BF16), earlier)
    turn = (iota((SLOTS, TOK), 0) % CAP).astype(F32)
    place = jnp.where(before == turn, hit, 0.0).astype(BF16)
    return place, nt(place, ids_t.astype(BF16))


def normalize(comp, gain):
    mean = jnp.mean(comp * comp, -1, keepdims=True)
    return (comp * lax.rsqrt(mean + 1e-06) * gain).astype(BF16)


def slot_weights(normed, router, slot_ids):
    scores = jax.nn.sigmoid(nn(normed, router))
    lane = iota((SLOTS, EXPERTS), 1)
    lane_f = lane.astype(F32)
    picked = jnp.zeros((SLOTS, EXPERTS), F32)
    for k in range(TOP):
        picked = jnp.where(slot_ids[:, k : k + 1] == lane_f, 1.0, picked)
    total = jnp.sum(scores * picked, -1, keepdims=True)
    own = jnp.sum(
        jnp.where(lane == iota((SLOTS, EXPERTS), 0) // CAP, scores, 0.0), -1, keepdims=True
    )
    return SCALE * own / total


def kernel(
    held, incoming, ids, gain, router, wg, wu, wd, out,
    xv, xp, idv, idp, gv, rv, wgu, wdv,
    zsend, zrecv, xa, xb, rsend, rrecv, guf, hbuf, oa, ob, pa, pb, of, bsend, brecv,
    wsend, wrecv, yv, b1, ov, comp_s, comp1_s,
    loc, snd, rcv,
):
    xbuf, osend, orecv = (xa, xb), (oa, ob), (pa, pb)
    sec = lax.axis_index("section")
    ex = lax.axis_index("expert")
    z, x = ex // SUB, ex % SUB
    e, zz = z // SUB, z % SUB

    def at_z(other):
        return {"expert": other * SUB + x}

    def at_x(other):
        return {"expert": z * SUB + other}

    def at_next(other):
        return {"section": (sec + 1) % NSEC, "expert": other * SUB + x}

    def at_previous(other):
        return {"section": (sec + NSEC - 1) % NSEC, "expert": other * SUB + x}

    after = at_next(z)

    flip = 1 - 2 * (sec % 2)

    def turn(k):
        step = jnp.where(k % 2 == 1, 8 - k // 2, k // 2 - 8)
        return (z + flip * step + NZ) % NZ

    def local(src, dst, number):
        return pltpu.make_async_copy(src, dst, loc.at[number])

    def send(src, dst, number, device):
        pltpu.make_async_remote_copy(
            src_ref=src, dst_ref=dst, send_sem=snd.at[number], recv_sem=rcv.at[number],
            device_id=device, device_id_type=MESH,
        ).start()

    def arrived(ref, number):
        pltpu.make_async_copy(ref, ref, rcv.at[number]).wait()

    def sent(ref, number):
        pltpu.make_async_copy(ref, ref, snd.at[number]).wait()

    barrier = pltpu.get_barrier_semaphore()

    @pl.loop(1, NZ)
    def _(k):
        pl.semaphore_signal(barrier, inc=1, device_id=at_z((z + k) % NZ), device_id_type=MESH)

    @pl.loop(0, NZ)
    def _(k):
        pl.semaphore_signal(barrier, inc=1, device_id=at_previous((z + k) % NZ), device_id_type=MESH)

    for k in range(1, SUB):
        pl.semaphore_signal(barrier, inc=1, device_id=at_x((x + k) % SUB), device_id_type=MESH)

    own = pl.ds(pl.multiple_of(zz * DS, 128), DS)
    starts = [
        local(held.at[0], xv, L_X),
        local(ids.at[:, 0], idv, L_IDS),
        local(gain, gv, L_GAIN),
        local(router.at[0], rv, L_ROUTER),
        local(wg.at[0, :, own], wgu.at[0, zz], L_WGU),
        local(wu.at[0, :, own], wgu.at[1, zz], L_WGU),
        local(wd.at[0, :, own], wdv.at[zz], L_WD),
    ]
    for copy in starts:
        copy.start()

    local(ids.at[:, 0], idv, L_IDS).wait()
    place0, slot_ids0 = placing(idv[0])
    pl.semaphore_wait(barrier, NZ - 1 + SUB - 1 + NZ)

    def exchange(source, target, number):
        for k in (2, 1, 3):
            to = (zz + k) % SUB
            columns = pl.ds(pl.multiple_of(to * DS, 128), DS)
            send(source.at[0, :, columns], target.at[zz], number, at_z(e * SUB + to))

    exchange(wg, wgu.at[0], S_WGU)
    local(gain, gv, L_GAIN).wait()
    gain_row = gv[...].astype(F32)
    local(held.at[0], xv, L_X).wait()
    low4 = iota((1, 8, 128), 1) < 4

    def pairs(get, zeros, half):
        evens, odds = [], []
        for v in range(2):
            block = BLOCKS[half][0] + 2 * v
            a = get(block)
            b = get(block + 1) if block + 1 < LB else zeros
            evens.append(jnp.where(low4, a, swap_halves(b)))
            odds.append(jnp.where(low4, swap_halves(a), b))
        return evens, odds

    def to_all_z(source, target, number, onward=False):
        @pl.loop(1, NZ)
        def _(k):
            to = turn(k)
            device = at_next(to) if onward else at_z(to)
            send(source.at[to // 2, to % 2], target.at[z], number, device)

        if onward:
            send(source.at[z // 2, z % 2], target.at[z], number, after)
        else:
            target[z] = source[z // 2, z % 2]

    def dispatch(tick, normed):
        rows = normed.astype(F32)
        for half in range(2):
            for part in range(SUB):

                def get(block):
                    column = (part * LB + block) * 128
                    return rows[:, column : column + 128].reshape(2, 8, 128)

                evens, odds = pairs(get, jnp.zeros((2, 8, 128), F32), half)
                even = jnp.concatenate(evens, 1).astype(BF16)
                odd = jnp.concatenate(odds, 1).astype(BF16)
                for h in range(2):
                    for n, message in ((2 * h, even[h]), (2 * h + 1, odd[h])):
                        to = n * SUB + part
                        zsend[tick, half, to // 2, to % 2] = message
            to_all_z(zsend.at[tick, half], zrecv.at[tick, half], S_TICK + PER_TICK * tick + half)

    def relay():
        @pl.when(sec == NSEC - 1)
        def _():
            send(incoming.at[0], xp, S_X, after)

        @pl.when(sec != NSEC - 1)
        def _():
            send(held.at[0], xp, S_X, after)

    def layer(tick, meanwhile, finish):
        base = S_TICK + PER_TICK * tick
        for half in range(2):
            arrived(zrecv.at[tick, half, pl.ds(0, NZ - 1)], base + half)
            got = zrecv[tick, half].astype(F32).reshape(8, 2, 2, 8, 128)
            mine = xbuf[half].at[tick, x]
            for v in range(2):
                a, b = got[:, 0, v], got[:, 1, v]
                even = jnp.where(low4, a, swap_halves(b))
                mine[:, 2 * v * 128 : (2 * v + 1) * 128] = even.reshape(64, 128).astype(BF16)
                if BLOCKS[half][0] + 2 * v + 1 < LB:
                    odd = jnp.where(low4, swap_halves(a), b)
                    mine[:, (2 * v + 1) * 128 : (2 * v + 2) * 128] = odd.reshape(64, 128).astype(BF16)
            for k in range(1, SUB):
                send(mine, mine, base + 2 + half, at_x((x + k) % SUB))
        if tick == 0:
            local(wgu.at[:, zz], wgu.at[:, zz], L_WGU).wait()
            arrived(wgu.at[:, pl.ds(0, SUB - 1)], S_WGU)
            exchange(wd, wdv, S_WD)
        arrived(xbuf[0].at[tick, pl.ds(0, SUB - 1)], base + 2)
        low, high = HALF[0]
        guf[...] = nt(xbuf[0][tick].reshape(256, 512), wgu[:, :, :, low:high].reshape(512, 512))
        arrived(xbuf[1].at[tick, pl.ds(0, SUB - 1)], base + 3)
        low, high = HALF[1]
        rows = xbuf[1][tick].reshape(256, DS - 512)
        for half in range(2):
            for which in range(2):
                weight = wgu[which, 2 * half : 2 * half + 2, :, low:high].reshape(128, DS - 512)
                column = which * 256 + half * 128
                sums = guf[:, column : column + 128] + nt(rows, weight)
                guf[:, column : column + 128] = sums
                rsend[tick, half, :, :, which * 128 : which * 128 + 128] = sums.reshape(SUB, 64, 128).astype(BF16)
            for k in range(1, SUB):
                to = (zz + k) % SUB
                send(rsend.at[tick, half, to], rrecv.at[tick, half, zz], base + 4 + half, at_z(e * SUB + to))
        if tick == 0:
            relay()
        mine = pl.ds(pl.multiple_of(zz * 64, 64), 64)
        for half in range(2):
            arrived(rrecv.at[tick, half, pl.ds(0, SUB - 1)], base + 4 + half)
            gate = guf[mine, half * 128 : half * 128 + 128]
            upper = guf[mine, 256 + half * 128 : 256 + half * 128 + 128]
            for k in range(1, SUB):
                other = rrecv[tick, half, (zz + k) % SUB].astype(F32)
                gate = gate + other[:, :128]
                upper = upper + other[:, 128:]
            hbuf[tick, half, zz] = (jax.nn.silu(gate) * upper).astype(BF16)
            for k in range(1, SUB):
                send(hbuf.at[tick, half, zz], hbuf.at[tick, half, zz], base + 6 + half, at_z(e * SUB + (zz + k) % SUB))
        if tick == 0:
            local(wd.at[0, :, own], wdv.at[zz], L_WD).wait()
            arrived(wdv.at[pl.ds(0, SUB - 1)], S_WD)
        for half in range(2):
            arrived(hbuf.at[tick, half, pl.ds(0, SUB - 1)], base + 6 + half)
        hidden = jnp.concatenate([hbuf[tick, 0].reshape(256, 128), hbuf[tick, 1].reshape(256, 128)], 1)
        for half in range(2):
            low, high = HALF[half]
            product = nn(hidden, wdv[:, :, low:high].reshape(256, high - low)).reshape(SUB, 64, high - low)
            osend[half][tick] = product.astype(BF16)
            of[:, :, low:high] = product
            for k in range(1, SUB):
                to = (x + k) % SUB
                send(osend[half].at[tick, to], orecv[half].at[tick, x], base + 8 + half, at_x(to))
        for half in range(2):
            low, high = HALF[half]
            arrived(orecv[half].at[tick, pl.ds(0, SUB - 1)], base + 8 + half)
            total = of[x, :, low:high]
            for k in range(1, SUB):
                total = total + orecv[half][tick, (x + k) % SUB].astype(F32)

            def get(block):
                column = block * 128 - low
                return total[:, column : column + 128].reshape(8, 8, 128)

            evens, odds = pairs(get, jnp.zeros((8, 8, 128), F32), half)
            bsend[tick, half, :, 0] = jnp.concatenate(evens, 1).astype(BF16)
            bsend[tick, half, :, 1] = jnp.concatenate(odds, 1).astype(BF16)
            to_all_z(bsend.at[tick, half], brecv.at[tick, half], base + 10 + half, tick == 0)
        meanwhile()
        for half in range(2):
            low, high = HALF[half]
            arrived(brecv.at[tick, half, pl.ds(0, NZ - tick)], base + 10 + half)
            for part in range(SUB):
                rows = [brecv[tick, half, n * SUB + part].astype(F32).reshape(2, 8, 128) for n in range(4)]
                blocks = []
                for v in range(2):
                    top = [jnp.where(low4[0], rows[2 * h][v], swap_halves(rows[2 * h + 1][v])) for h in range(2)]
                    blocks.append(jnp.concatenate(top, 0))
                    if BLOCKS[half][0] + 2 * v + 1 < LB:
                        top = [jnp.where(low4[0], swap_halves(rows[2 * h][v]), rows[2 * h + 1][v]) for h in range(2)]
                        blocks.append(jnp.concatenate(top, 0))
                finish(half, part, slice(part * DS + low, part * DS + high), jnp.concatenate(blocks, 1))

    normed = normalize(nn(place0, xv[...]), gain_row)
    dispatch(0, normed)
    exchange(wu, wgu.at[1], S_WGU)
    send(idv.at[0], idp, S_IDS, after)
    local(router.at[0], rv, L_ROUTER).wait()
    wsend[...] = jnp.broadcast_to(slot_weights(normed, rv[...], slot_ids0), (SLOTS, 128))
    send(wsend, wrecv, S_Y, after)
    place1, slot_ids1 = placing(idv[1])
    known = {}

    def prepare():
        arrived(idp, S_IDS)
        prev, _ = placing(idp[...])
        lower = one_hot(iota((SLOTS, SLOTS), 1) < iota((SLOTS, SLOTS), 0))
        live = jnp.where(sec == 0, 0.0, 1.0)
        unique = jnp.where(nn(lower, prev) == 0.0, prev.astype(F32), 0.0) * live
        touched = jnp.sum(unique, 0, keepdims=True)
        untouched = (place1.astype(F32) * (1.0 - touched)).astype(BF16)
        unique = unique.astype(BF16)
        known["moved"] = nt(place1, unique).astype(BF16)
        eye = one_hot(iota((TOK, TOK), 0) == iota((TOK, TOK), 1))
        known["scatter"] = nt(eye, unique).astype(BF16)
        known["combine"] = nt(eye, jnp.concatenate([place1, place1], 0)).astype(BF16)
        known["kept"] = 1.0 - jnp.sum(known["scatter"].astype(F32), 1, keepdims=True)
        same = nt(prev, prev).astype(BF16)
        known["same"] = jnp.concatenate([same, same], 1)
        arrived(wrecv, S_Y)
        known["weights"] = wrecv[:, :1]
        arrived(xp, S_X)
        comp_s[...] = nn(prev, xp[...])
        comp1_s[...] = nn(untouched, xp[...])

    def changed(half, part, columns, moe):
        rows = comp_s[:, columns] + nn(known["same"], halves(moe * known["weights"]))
        yv[:, columns] = rows.astype(BF16)
        comp1_s[:, columns] += nn(known["moved"], yv[:, columns])

    layer(0, prepare, changed)
    kept, scatter, combine = known["kept"], known["scatter"], known["combine"]
    normed = normalize(comp1_s[...], gain_row)
    dispatch(1, normed)
    weights1 = slot_weights(normed, rv[...], slot_ids1)

    def block():
        for part in range(SUB):
            columns = slice(part * DS, (part + 1) * DS)
            b1[:, columns] = xp[:, columns].astype(F32) * kept + nn(scatter, yv[:, columns])

    outs = []

    def result(half, part, columns, moe):
        ov[:, columns] = (b1[:, columns] + nn(combine, halves(moe * weights1))).astype(BF16)
        copy = local(ov.at[:, columns], out.at[0, :, columns], L_OUT + SUB * half + part)
        copy.start()
        outs.append(copy)

    layer(1, block, result)
    sent(wgu.at[:, pl.ds(0, SUB - 1)], S_WGU)
    sent(wdv.at[pl.ds(0, SUB - 1)], S_WD)
    sent(xp, S_X)
    sent(idp, S_IDS)
    sent(wrecv, S_Y)
    for half in range(2):
        for tick in range(2):
            base = S_TICK + PER_TICK * tick + half
            sent(zrecv.at[tick, half, pl.ds(0, NZ - 1)], base)
            sent(xbuf[half].at[tick, pl.ds(0, SUB - 1)], base + 2)
            sent(rrecv.at[tick, half, pl.ds(0, SUB - 1)], base + 4)
            sent(hbuf.at[tick, half, pl.ds(0, SUB - 1)], base + 6)
            sent(orecv[half].at[tick, pl.ds(0, SUB - 1)], base + 8)
            sent(brecv.at[tick, half, pl.ds(0, NZ - tick)], base + 10)
    for copy in outs:
        copy.wait()


def body(held, incoming, route_ids, gain, router, w_gate, w_up, w_down):
    any_space = pl.BlockSpec(memory_space=pltpu.HBM)
    vm = pltpu.VMEM
    return pl.pallas_call(
        kernel,
        out_shape=jax.ShapeDtypeStruct((1, TOK, D), BF16),
        in_specs=[any_space] * 8,
        out_specs=any_space,
        scratch_shapes=[
            vm((TOK, D), BF16),
            vm((TOK, D), BF16),
            vm((2, TOP, TOK), jnp.int32),
            vm((TOP, TOK), jnp.int32),
            vm((1, D), BF16),
            vm((D, EXPERTS), BF16),
            vm((2, SUB, UNITS, DS), BF16),
            vm((SUB, UNITS, DS), BF16),
            vm((2, 2, 8, 2, 16, 128), BF16),
            vm((2, 2, NZ, 16, 128), BF16),
            vm((2, SUB, 64, 512), BF16),
            vm((2, SUB, 64, DS - 512), BF16),
            vm((2, 2, SUB, 64, 256), BF16),
            vm((2, 2, SUB, 64, 256), BF16),
            vm((256, 512), F32),
            vm((2, 2, SUB, 64, 128), BF16),
            vm((2, SUB, 64, 512), BF16),
            vm((2, SUB, 64, DS - 512), BF16),
            vm((2, SUB, 64, 512), BF16),
            vm((2, SUB, 64, DS - 512), BF16),
            vm((SUB, 64, DS), F32),
            vm((2, 2, 8, 2, 16, 128), BF16),
            vm((2, 2, NZ, 16, 128), BF16),
            vm((SLOTS, 128), F32),
            vm((SLOTS, 128), F32),
            vm((SLOTS, D), BF16),
            vm((TOK, D), F32),
            vm((TOK, D), BF16),
            vm((SLOTS, D), F32),
            vm((SLOTS, D), F32),
            pltpu.SemaphoreType.DMA((L_OUT + 2 * SUB,)),
            pltpu.SemaphoreType.DMA((N_SEM,)),
            pltpu.SemaphoreType.DMA((N_SEM,)),
        ],
        compiler_params=pltpu.CompilerParams(
            collective_id=0, has_side_effects=True, vmem_limit_bytes=60 * 1024 * 1024
        ),
    )(held, incoming, jnp.swapaxes(route_ids, 2, 3), gain, router, w_gate, w_up, w_down)


def solution(mesh):
    return jax.shard_map(
        body,
        mesh=mesh,
        in_specs=(
            P("section", "expert", None),
            P(None, "expert", None),
            P(None, "section", "expert", None),
            P("section", None),
            P("section", None, None),
            P("section", "expert", None),
            P("section", "expert", None),
            P("section", "expert", None),
        ),
        out_specs=P("section", "expert", None),
        check_vma=False,
    )
```

time: 148 us -> 128 us (0.86)
  the two profiles are of different devices: /device:TPU:24 before, /device:TPU:16 now
where the time goes in v2:
time: 128 us
  Pallas kernels  126 us (98%)
  local copies, waits for them, and re-layouts  2.16 us (2%)
    pallas_call x1, Pallas kernels, body(): pl.pallas_call(kernel, out_shape=jax.ShapeDtypeStruct((1, TOK, D), BF16),...  126 us

profile of v2, /device:TPU:16, one launch (start us, length us, event | category | flops | bytes accessed | tf_op | source)
XLA Modules:
  0.0 127.9 jit_solution(8063585660671830598)
XLA Ops:
  0.0 125.7 %shard_map.82 = bf16[1,128,3584]{2,1,0:T(8,128)(2,1)} custom-call(bf16[1,128,3584]{2,1,0:T(8,128)(2,1)} %held.1, bf16[1,128,3584]{2,1,0:T(8,128)(2,1)} %incoming.1, s32[2,1,8,128]{3,2,1,0:T(8,128)} %bitcast.1, bf16[1,3584]{1,0:T(2,128)(2,1)} %gain.1, bf16[1,3584,256]{2,1,0:T(8,128)(2,1)} %router.1, bf16[1,64,3584]{2,1,0:T(8,128)(2,1)} %wg.1, ...), custom_call_target="tpu_custom_call" | custom-call | tf_op jit(solution)/shard_map/pallas_call | solution.py:403
  125.7 2.2 %copy.10 = bf16[1,128,3584]{2,1,0:T(8,128)(2,1)} copy(bf16[1,128,3584]{2,1,0:T(8,128)(2,1)} %shard_map.82) | data formatting | bytes 1835008

commit v3 on v2

--- a/solution.py
+++ b/solution.py
@@ -118,6 +118,7 @@
     after = at_next(z)
 
     flip = 1 - 2 * (sec % 2)
+    far_first = 2, 2 - flip, 2 + flip
 
     def turn(k):
         step = jnp.where(k % 2 == 1, 8 - k // 2, k // 2 - 8)
@@ -229,7 +230,7 @@
         def _():
             send(held.at[0], xp, S_X, after)
 
-    def layer(tick, meanwhile, finish):
+    def layer(tick, meanwhile, later, finish):
         base = S_TICK + PER_TICK * tick
         for half in range(2):
             arrived(zrecv.at[tick, half, pl.ds(0, NZ - 1)], base + half)
@@ -242,12 +243,11 @@
                 if BLOCKS[half][0] + 2 * v + 1 < LB:
                     odd = jnp.where(low4, swap_halves(a), b)
                     mine[:, (2 * v + 1) * 128 : (2 * v + 2) * 128] = odd.reshape(64, 128).astype(BF16)
-            for k in range(1, SUB):
+            for k in far_first:
                 send(mine, mine, base + 2 + half, at_x((x + k) % SUB))
         if tick == 0:
             local(wgu.at[:, zz], wgu.at[:, zz], L_WGU).wait()
             arrived(wgu.at[:, pl.ds(0, SUB - 1)], S_WGU)
-            exchange(wd, wdv, S_WD)
         arrived(xbuf[0].at[tick, pl.ds(0, SUB - 1)], base + 2)
         low, high = HALF[0]
         guf[...] = nt(xbuf[0][tick].reshape(256, 512), wgu[:, :, :, low:high].reshape(512, 512))
@@ -261,7 +261,7 @@
                 sums = guf[:, column : column + 128] + nt(rows, weight)
                 guf[:, column : column + 128] = sums
                 rsend[tick, half, :, :, which * 128 : which * 128 + 128] = sums.reshape(SUB, 64, 128).astype(BF16)
-            for k in range(1, SUB):
+            for k in far_first:
                 to = (zz + k) % SUB
                 send(rsend.at[tick, half, to], rrecv.at[tick, half, zz], base + 4 + half, at_z(e * SUB + to))
         if tick == 0:
@@ -276,7 +276,7 @@
                 gate = gate + other[:, :128]
                 upper = upper + other[:, 128:]
             hbuf[tick, half, zz] = (jax.nn.silu(gate) * upper).astype(BF16)
-            for k in range(1, SUB):
+            for k in far_first:
                 send(hbuf.at[tick, half, zz], hbuf.at[tick, half, zz], base + 6 + half, at_z(e * SUB + (zz + k) % SUB))
         if tick == 0:
             local(wd.at[0, :, own], wdv.at[zz], L_WD).wait()
@@ -289,9 +289,10 @@
             product = nn(hidden, wdv[:, :, low:high].reshape(256, high - low)).reshape(SUB, 64, high - low)
             osend[half][tick] = product.astype(BF16)
             of[:, :, low:high] = product
-            for k in range(1, SUB):
+            for k in far_first:
                 to = (x + k) % SUB
                 send(osend[half].at[tick, to], orecv[half].at[tick, x], base + 8 + half, at_x(to))
+        meanwhile()
         for half in range(2):
             low, high = HALF[half]
             arrived(orecv[half].at[tick, pl.ds(0, SUB - 1)], base + 8 + half)
@@ -307,7 +308,7 @@
             bsend[tick, half, :, 0] = jnp.concatenate(evens, 1).astype(BF16)
             bsend[tick, half, :, 1] = jnp.concatenate(odds, 1).astype(BF16)
             to_all_z(bsend.at[tick, half], brecv.at[tick, half], base + 10 + half, tick == 0)
-        meanwhile()
+        later()
         for half in range(2):
             low, high = HALF[half]
             arrived(brecv.at[tick, half, pl.ds(0, NZ - tick)], base + 10 + half)
@@ -325,42 +326,42 @@
     normed = normalize(nn(place0, xv[...]), gain_row)
     dispatch(0, normed)
     exchange(wu, wgu.at[1], S_WGU)
+    exchange(wd, wdv, S_WD)
     send(idv.at[0], idp, S_IDS, after)
     local(router.at[0], rv, L_ROUTER).wait()
     wsend[...] = jnp.broadcast_to(slot_weights(normed, rv[...], slot_ids0), (SLOTS, 128))
     send(wsend, wrecv, S_Y, after)
     place1, slot_ids1 = placing(idv[1])
-    known = {}
+
+    arrived(idp, S_IDS)
+    prev, _ = placing(idp[...])
+    lower = one_hot(iota((SLOTS, SLOTS), 1) < iota((SLOTS, SLOTS), 0))
+    live = jnp.where(sec == 0, 0.0, 1.0)
+    unique = jnp.where(nn(lower, prev) == 0.0, prev.astype(F32), 0.0) * live
+    touched = jnp.sum(unique, 0, keepdims=True)
+    untouched = (place1.astype(F32) * (1.0 - touched)).astype(BF16)
+    unique = unique.astype(BF16)
+    moved = nt(place1, unique).astype(BF16)
+    eye = one_hot(iota((TOK, TOK), 0) == iota((TOK, TOK), 1))
+    scatter = nt(eye, unique).astype(BF16)
+    combine = nt(eye, jnp.concatenate([place1, place1], 0)).astype(BF16)
+    kept = 1.0 - jnp.sum(scatter.astype(F32), 1, keepdims=True)
+    same = nt(prev, prev).astype(BF16)
+    same = jnp.concatenate([same, same], 1)
 
     def prepare():
-        arrived(idp, S_IDS)
-        prev, _ = placing(idp[...])
-        lower = one_hot(iota((SLOTS, SLOTS), 1) < iota((SLOTS, SLOTS), 0))
-        live = jnp.where(sec == 0, 0.0, 1.0)
-        unique = jnp.where(nn(lower, prev) == 0.0, prev.astype(F32), 0.0) * live
-        touched = jnp.sum(unique, 0, keepdims=True)
-        untouched = (place1.astype(F32) * (1.0 - touched)).astype(BF16)
-        unique = unique.astype(BF16)
-        known["moved"] = nt(place1, unique).astype(BF16)
-        eye = one_hot(iota((TOK, TOK), 0) == iota((TOK, TOK), 1))
-        known["scatter"] = nt(eye, unique).astype(BF16)
-        known["combine"] = nt(eye, jnp.concatenate([place1, place1], 0)).astype(BF16)
-        known["kept"] = 1.0 - jnp.sum(known["scatter"].astype(F32), 1, keepdims=True)
-        same = nt(prev, prev).astype(BF16)
-        known["same"] = jnp.concatenate([same, same], 1)
+        arrived(xp, S_X)
+        both = nn(jnp.concatenate([prev, untouched], 0), xp[...])
+        comp_s[...] = both[:SLOTS]
+        comp1_s[...] = both[SLOTS:]
         arrived(wrecv, S_Y)
-        known["weights"] = wrecv[:, :1]
-        arrived(xp, S_X)
-        comp_s[...] = nn(prev, xp[...])
-        comp1_s[...] = nn(untouched, xp[...])
 
     def changed(half, part, columns, moe):
-        rows = comp_s[:, columns] + nn(known["same"], halves(moe * known["weights"]))
+        rows = comp_s[:, columns] + nn(same, halves(moe * wrecv[:, :1]))
         yv[:, columns] = rows.astype(BF16)
-        comp1_s[:, columns] += nn(known["moved"], yv[:, columns])
-
-    layer(0, prepare, changed)
-    kept, scatter, combine = known["kept"], known["scatter"], known["combine"]
+        comp1_s[:, columns] += nn(moved, yv[:, columns])
+
+    layer(0, prepare, lambda: None, changed)
     normed = normalize(comp1_s[...], gain_row)
     dispatch(1, normed)
     weights1 = slot_weights(normed, rv[...], slot_ids1)
@@ -378,7 +379,7 @@
         copy.start()
         outs.append(copy)
 
-    layer(1, block, result)
+    layer(1, block, lambda: None, result)
     sent(wgu.at[:, pl.ds(0, SUB - 1)], S_WGU)
     sent(wdv.at[pl.ds(0, SUB - 1)], S_WD)
     sent(xp, S_X)

time: 128 us -> 128 us (level)
  the two profiles are of different devices: /device:TPU:16 before, /device:TPU:18 now
where the time goes in v3:
time: 128 us; the launch traced here: 127 us
  Pallas kernels  125 us (98%)
  local copies, waits for them, and re-layouts  2.16 us (2%)
    pallas_call x1, Pallas kernels, body(): pl.pallas_call(kernel, out_shape=jax.ShapeDtypeStruct((1, TOK, D), BF16),...  125 us

profile of v3, /device:TPU:18, one launch (start us, length us, event | category | flops | bytes accessed | tf_op | source)
XLA Modules:
  0.0 127.4 jit_solution(4287369910633563908)
XLA Ops:
  0.0 125.2 %shard_map.82 = bf16[1,128,3584]{2,1,0:T(8,128)(2,1)} custom-call(bf16[1,128,3584]{2,1,0:T(8,128)(2,1)} %held.1, bf16[1,128,3584]{2,1,0:T(8,128)(2,1)} %incoming.1, s32[2,1,8,128]{3,2,1,0:T(8,128)} %bitcast.1, bf16[1,3584]{1,0:T(2,128)(2,1)} %gain.1, bf16[1,3584,256]{2,1,0:T(8,128)(2,1)} %router.1, bf16[1,64,3584]{2,1,0:T(8,128)(2,1)} %wg.1, ...), custom_call_target="tpu_custom_call" | custom-call | tf_op jit(solution)/shard_map/pallas_call | solution.py:404
  125.2 2.2 %copy.10 = bf16[1,128,3584]{2,1,0:T(8,128)(2,1)} copy(bf16[1,128,3584]{2,1,0:T(8,128)(2,1)} %shard_map.82) | data formatting | bytes 1835008
